TPU v7x, 32 devices: a whole 2x2x4 slice. The times are simulated.
32 devices in a mesh: copy: 4 (over y, x), row: 8 (over z, core).
Axes of the slice: x: 2, y: 2, z: 4, core: 2. Of those that a mesh axis runs over, the one named last changes fastest.
Arguments:
- left_proj: bfloat16 [128, 40, 1536], P(None, 'row', 'copy'), may hold values from -6 to 6
- left_gate: bfloat16 [128, 40, 1536], P(None, 'row', 'copy'), may hold values from -8 to 8
- right_factor: bfloat16 [128, 384, 1536], P(None, 'row', 'copy'), may hold values from -6 to 6
- cotangent: bfloat16 [128, 40, 1536], P(None, 'row', 'copy'), may hold values from -0.15625 to 0.15625
- residue_mask: int32 [384], replicated, may hold values 0 or 1
Outputs:
- grad_proj: bfloat16 [128, 40, 1536], P(None, 'row', 'copy')
- grad_gate: bfloat16 [128, 40, 1536], P(None, 'row', 'copy')
- grad_right: bfloat16 [128, 384, 1536], P(None, 'row', 'copy')
Inputs may be any that keep to these rules, and one draw needn't show every extreme that they name: `residue_mask`: 1 marks a present residue, 0 a missing one.
All inputs are finite; a program needn't handle non-finite values.
Results may differ from a plain program's by a relative error of at most 0.0049.
Values may be sent and summed in bfloat16 or wider, within the bound.
A program may use at most 64 MiB of HBM per device.

v0:
```python
import jax
import jax.numpy as jnp
from jax import lax
from jax.sharding import PartitionSpec as P


def on_device(left_proj, left_gate, right_factor, cotangent, residue_mask):
    copies = lax.axis_size("copy")
    copy_here = lax.axis_index("copy")
    row_here = lax.axis_index("row")
    row_count = left_proj.shape[1]
    keep_rows = lax.dynamic_slice_in_dim(residue_mask, row_here * row_count, row_count).astype(
        jnp.float32
    )
    keep_cols = residue_mask.astype(jnp.float32)
    keep_both = keep_rows[None, :, None] * keep_cols[None, None, :]
    opened = jax.nn.sigmoid(left_gate.astype(jnp.float32))
    left_factor = (keep_both * opened * left_proj.astype(jnp.float32)).astype(jnp.bfloat16)
    cot_local, left_local, right_local = (
        lax.all_to_all(cotangent, "row", split_axis=0, concat_axis=1, tiled=True),
        lax.all_to_all(left_factor, "row", split_axis=0, concat_axis=1, tiled=True),
        lax.all_to_all(right_factor, "row", split_axis=0, concat_axis=1, tiled=True),
    )
    cot_copies = lax.all_gather(cot_local[None], "copy", axis=0, tiled=True)

    def cot_block(offset):
        return lax.dynamic_index_in_dim(cot_copies, offset % copies, 0, keepdims=False)

    zero_left = jnp.zeros(cot_local.shape, jnp.float32)
    zero_right = jnp.zeros(right_local.shape, jnp.float32)
    pieces = (
        lax.all_gather(left_local[None], "copy", axis=0, tiled=True),
        lax.all_gather(right_local[None], "copy", axis=0, tiled=True),
    )
    first = jnp.int32(0)
    left_total = zero_left
    for number in range(pieces[1].shape[0]):
        source = first + number
        left_total = left_total + jnp.einsum(
            "cij,cjk->cik",
            cot_block(copy_here - source),
            pieces[1][number],
            preferred_element_type=jnp.float32,
        )
    right_totals = zero_right
    left_piece = pieces[0]
    for number in range(left_piece.shape[0]):
        source = first + number
        right_totals = right_totals + jnp.einsum(
            "cij,cik->cjk",
            cot_block(source - copy_here),
            left_piece[number],
            preferred_element_type=jnp.float32,
        )
    rows_left, rows_right = (
        lax.all_to_all(
            left_total.astype(jnp.bfloat16), "row", split_axis=1, concat_axis=0, tiled=True
        ),
        lax.all_to_all(
            right_totals.astype(jnp.bfloat16), "row", split_axis=1, concat_axis=0, tiled=True
        ),
    )
    left_wide = rows_left.astype(jnp.float32)
    grad_proj = (left_wide * keep_both * opened).astype(jnp.bfloat16)
    grad_gate = (
        left_wide * keep_both * left_proj.astype(jnp.float32) * opened * (1.0 - opened)
    ).astype(jnp.bfloat16)
    return (grad_proj, grad_gate, rows_right)


def solution(mesh):
    in_specs = (
        P(None, "row", "copy"),
        P(None, "row", "copy"),
        P(None, "row", "copy"),
        P(None, "row", "copy"),
        P(),
    )
    out_specs = (P(None, "row", "copy"), P(None, "row", "copy"), P(None, "row", "copy"))
    return jax.shard_map(
        on_device, mesh=mesh, in_specs=in_specs, out_specs=out_specs, check_vma=False
    )
```

profile of v0, /device:TPU:0, one launch (start us, length us, event | category | flops | bytes accessed | tf_op | source)
XLA Modules:
  0.0 566.3 jit_solution(5734403837097731216)
XLA Ops:
  7.2 1.3 copy.40
  8.5 27.1 %all_to_all.72 = bf16[128,5,384]{2,1,0:T(8,128)(2,1)S(1)} all-to-all(bf16[128,5,384]{2,1,0:T(8,128)(2,1)S(1)} %copy.40), channel_id=1, replica_groups=mesh['copy'=4,'row'=8] {'row'}, dimensions={0} | all-to-all | bytes 983040 | tf_op jit(solution)/shard_map/all_to_all | solution.py:20
  35.6 4.6 all-to-all-start.1
  40.2 0.0 all-gather.4.cloned.1.call-start
  40.3 0.1 copy.42
  40.3 0.9 copy.43
  41.2 0.0 all-gather.4.cloned.1.call-update
  41.2 0.0 all-gather.6.cloned.1.call-start
  41.3 104.2 %all-to-all-done.1 = bf16[128,48,384]{2,1,0:T(8,128)(2,1)} async-done(((bf16[128,48,384]{2,1,0:T(8,128)(2,1)}), bf16[128,48,384]{2,1,0:T(8,128)(2,1)}, u32[]{:S(2)}, u32[]{:S(2)}) %all-to-all-start.1) | async-done | bytes 4718624 | tf_op jit(solution)/shard_map/all_to_all | solution.py:22
  145.5 5.2 copy.44
  150.7 0.0 all-gather.6.cloned.1.call-update
  150.8 0.0 all-gather.4.cloned.1.call-done
  150.8 0.0 copy-start
  150.9 174.9 %all-gather.6.cloned.1.call-done = bf16[4,16,384,384]{3,2,1,0:T(8,128)(2,1)} async-done(((bf16[1,16,384,384]{3,2,1,0:T(8,128)(2,1)}), bf16[4,16,384,384]{3,2,1,0:T(8,128)(2,1)}) %all-gather.6.cloned.1.call-update) | async-done | bytes 18874384 | tf_op jit(solution)/shard_map/all_gather | solution.py:33
  325.7 3.3 fusion.2
  329.1 0.0 copy-done
  329.1 3.2 fusion.4
  332.3 3.2 fusion.5
  335.5 0.0 copy-start.4
  335.5 0.0 copy-start.2
  335.6 0.0 copy-start.3
  335.6 3.3 fusion.7
  338.9 0.8 copy.45
  339.7 4.6 all-to-all-start.2
  344.3 0.0 all-gather.8.cloned.1.call-start
  344.4 0.0 copy-done.4
  344.4 0.1 dynamic-slice_convert_fusion
  344.5 0.1 broadcast_multiply_fusion
  344.6 14.4 %all-to-all-done.2 = bf16[16,40,384]{2,0,1:T(8,128)(2,1)S(1)} async-done(((bf16[16,40,384]{2,0,1:T(8,128)(2,1)}), bf16[16,40,384]{2,0,1:T(8,128)(2,1)S(1)}, u32[]{:S(2)}, u32[]{:S(2)}) %all-to-all-start.2) | async-done | bytes 491552 | tf_op jit(solution)/shard_map/all_to_all | solution.py:56
  359.0 0.1 convert_bitcast_fusion
  359.1 0.1 copy.46
  359.1 0.0 copy-done.2
  359.2 0.0 copy-done.3
  359.2 1.5 fusion.10
  360.7 0.3 copy.47
  361.0 23.4 %all_to_all.73 = bf16[128,5,384]{2,1,0:T(8,128)(2,1)S(1)} all-to-all(bf16[128,5,384]{2,1,0:T(8,128)(2,1)S(1)} %copy.47), channel_id=1, replica_groups=mesh['copy'=4,'row'=8] {'row'}, dimensions={0} | all-to-all | bytes 983040 | tf_op jit(solution)/shard_map/all_to_all | solution.py:21
  384.4 0.1 copy.49
  384.4 0.9 copy.50
  385.3 0.0 all-gather.8.cloned.1.call-update
  385.4 32.2 %all-gather.8.cloned.1.call-done = bf16[4,16,40,384]{3,2,1,0:T(8,128)(2,1)} async-done(((bf16[1,16,40,384]{3,2,1,0:T(8,128)(2,1)}), bf16[4,16,40,384]{3,2,1,0:T(8,128)(2,1)}) %all-gather.8.cloned.1.call-update) | async-done | bytes 1966096 | tf_op jit(solution)/shard_map/all_gather | solution.py:32
  417.6 2.6 fusion.12
  420.3 0.0 copy-done.1
  420.3 5.1 fusion.13
  425.4 5.1 fusion.14
  430.5 11.1 %add_convert_fusion = bf16[16,384,384]{2,1,0:T(8,128)(2,1)} fusion(f32[16,384,384]{2,1,0:T(8,128)S(1)} %fusion.12, f32[16,384,384]{2,1,0:T(8,128)} %fusion.14, f32[16,384,384]{2,1,0:T(8,128)} %fusion.13, bf16[4,16,40,384]{3,2,1,0:T(8,128)(2,1)} %all-gather.8.cloned.1.call-done, bf16[4,16,40,384]{3,2,1,0:T(8,128)(2,1)S(1)} %copy-done, s32[]{:T(128)S(6)} %select_n.79), kind=kOutput, calls=%fused_computation | convolution fusion | flops 198180864 | bytes 34013188 | tf_op jit(solution)/shard_map/cij,cik->cjk/dot_general | solution.py:49
  441.6 5.1 copy.51
  446.8 109.7 %all_to_all.74 = bf16[16,384,384]{2,0,1:T(8,128)(2,1)S(1)} all-to-all(bf16[16,384,384]{2,0,1:T(8,128)(2,1)S(1)} %copy.51), channel_id=1, replica_groups=mesh['copy'=4,'row'=8] {'row'}, dimensions={1} | all-to-all | bytes 9437184 | tf_op jit(solution)/shard_map/all_to_all | solution.py:59
  556.5 3.3 copy.52
  (2 shorter events, 0.0 us)
Async XLA Ops:
  35.6 109.9 %all-to-all-start.1 = ((bf16[128,48,384]{2,1,0:T(8,128)(2,1)}), bf16[128,48,384]{2,1,0:T(8,128)(2,1)}, u32[]{:S(2)}, u32[]{:S(2)}) async-start(bf16[128,48,384]{2,1,0:T(8,128)(2,1)} %param.7), calls=%async_computation.1 | async-start | bytes 9437184 | tf_op jit(solution)/shard_map/all_to_all | solution.py:22
  40.2 110.6 %all-gather.4.cloned.1.call-start = ((), (), s32[]{:S(2)}) async-start(), calls=%async_computation.5 | async-start | bytes 2457600 | tf_op jit(solution)/shard_map/all_gather | solution.py:24
  41.2 284.5 %all-gather.6.cloned.1.call-start = ((), (), s32[]{:S(2)}) async-start(), calls=%async_computation.6 | async-start | bytes 23592960 | tf_op jit(solution)/shard_map/all_gather | solution.py:33
  150.8 178.2 %copy-start = (bf16[4,16,40,384]{3,2,1,0:T(8,128)(2,1)S(1)}, bf16[4,16,40,384]{3,2,1,0:T(8,128)(2,1)}, u32[]{:S(2)}) copy-start(bf16[4,16,40,384]{3,2,1,0:T(8,128)(2,1)} %all-gather.4.cloned.1.call-done) | copy-start | bytes 5898244
  335.5 8.9 %copy-start.4 = (s32[384]{0:T(512)S(1)}, s32[384]{0:T(512)}, u32[]{:S(2)}) copy-start(s32[384]{0:T(512)} %param.9) | copy-start | bytes 4612
  335.5 23.6 %copy-start.2 = (bf16[128,5,384]{2,0,1:T(8,128)(2,1)S(1)}, bf16[128,5,384]{2,0,1:T(8,128)(2,1)}, u32[]{:S(2)}) copy-start(bf16[128,5,384]{2,0,1:T(8,128)(2,1)} %param.5) | copy-start | bytes 1474564
  335.6 23.6 %copy-start.3 = (bf16[128,5,384]{2,0,1:T(8,128)(2,1)S(1)}, bf16[128,5,384]{2,0,1:T(8,128)(2,1)}, u32[]{:S(2)}) copy-start(bf16[128,5,384]{2,0,1:T(8,128)(2,1)} %param.6) | copy-start | bytes 1474564
  339.7 19.3 %all-to-all-start.2 = ((bf16[16,40,384]{2,0,1:T(8,128)(2,1)}), bf16[16,40,384]{2,0,1:T(8,128)(2,1)S(1)}, u32[]{:S(2)}, u32[]{:S(2)}) async-start(bf16[16,40,384]{2,0,1:T(8,128)(2,1)} %copy.45), calls=%async_computation.2 | async-start | bytes 983040 | tf_op jit(solution)/shard_map/all_to_all | solution.py:56
  344.3 73.3 %all-gather.8.cloned.1.call-start = ((), (), s32[]{:S(2)}) async-start(), calls=%async_computation.7 | async-start | bytes 2457600 | tf_op jit(solution)/shard_map/all_gather | solution.py:32
  417.6 2.6 copy-start.1
Sparse Core Ops, SparseCore 0:
  43.5 35.5 all-gather.3
  150.9 174.8 all-gather.5
  385.5 32.1 all-gather.7
where the time goes:
time: 567 us; the launch traced here: 566 us
  waiting for transfers between devices  326 us (57%)
  blocking collectives  160 us (28%)
  matrix products  37.1 us (7%)
  local copies, waits for them, and re-layouts  18.1 us (3%)
  between operations  14.1 us (2%)
  starting transfers between devices  9.33 us (2%)
    all_gather x1, waiting for transfers between devices, on_device(): lax.all_gather(right_local[None], 'copy', axis=0, tiled=True)  175 us
    all_to_all x1, blocking collectives, on_device(): lax.all_to_all(right_totals.astype(jnp.bfloat16), 'row', split_axis=1, co...  110 us
    all_to_all x1, waiting for transfers between devices, on_device(): lax.all_to_all(right_factor, 'row', split_axis=0, concat_axis=1, tiled=True)  104 us
    all_gather x1, waiting for transfers between devices, on_device(): lax.all_gather(left_local[None], 'copy', axis=0, tiled=True)  32.2 us
    all_to_all x1, blocking collectives, on_device(): lax.all_to_all(cotangent, 'row', split_axis=0, concat_axis=1, tiled=True)  27.1 us
    dot_general x4, matrix products, on_device(): jnp.einsum('cij,cik->cjk', cot_block(source - copy_here), left_piece[numb...  24 us
    all_to_all x1, blocking collectives, on_device(): lax.all_to_all(left_factor, 'row', split_axis=0, concat_axis=1, tiled=True)  23.4 us
    all_to_all x1, waiting for transfers between devices, on_device(): lax.all_to_all(left_total.astype(jnp.bfloat16), 'row', split_axis=1, conc...  14.4 us
  transfers between devices with their start and end apart: 5, of which 4 were waited for; matrix products, arithmetic and copies ran while one was open for 1% of the time, Pallas kernels for 0%

commit v1 on v0

v1 whole, which is shorter than its diff:
```python
import jax
import jax.numpy as jnp
from jax import lax
from jax.experimental import pallas as pl
from jax.experimental.pallas import tpu as pltpu
from jax.sharding import PartitionSpec as P

MESH = pl.DeviceIdType.MESH
ANY = pl.BlockSpec(memory_space=pl.ANY)


def place(copies, rows):
    g, r = lax.axis_index("copy"), lax.axis_index("row")
    core = lax.rem(r, 2)
    return g, r, core, r + 1 - 2 * core


def greet(g, r, others):
    barrier = pltpu.get_barrier_semaphore()
    for device in others:
        pl.semaphore_signal(barrier, inc=1, device_id=device, device_id_type=MESH)
    pl.semaphore_wait(barrier, len(others))


def remote(src, dst, send, recv, device):
    return pltpu.make_async_remote_copy(
        src_ref=src, dst_ref=dst, send_sem=send, recv_sem=recv, device_id=device, device_id_type=MESH
    )


def spread(
    copies, rows, share,
    right, left, cot, right_all, left_all, cot_all,
    left_mid, cot_mid, own, mid_sems, cot_sems, right_sems, row_sems, pair_sems, cot_row_sems,
):
    g, r, core, sibling = place(copies, rows)
    chips = rows // 2
    greet(
        g, r,
        [(lax.rem(g + k, copies), r) for k in range(1, copies)]
        + [(g, lax.rem(r + k, rows)) for k in range(1, rows)],
    )
    local = [
        pltpu.make_async_copy(left.at[:, g], left_mid.at[g], own.at[0]),
        pltpu.make_async_copy(cot.at[g], cot_mid.at[g], own.at[1]),
        pltpu.make_async_copy(right.at[pl.ds(g * share, share)], right_all.at[:, g], own.at[2]),
    ]
    for copy in local:
        copy.start()
    mids, cots, rights = [], [], []
    for k in range(1, copies):
        q = lax.rem(g + k, copies)
        mids.append(remote(left.at[:, q], left_mid.at[g], mid_sems.at[0, k], mid_sems.at[1, k], (q, r)))
        cots.append(remote(cot.at[q], cot_mid.at[g], cot_sems.at[0, k], cot_sems.at[1, k], (q, r)))
        rights.append(
            remote(
                right.at[pl.ds(q * share, share)], right_all.at[:, g],
                right_sems.at[0, k], right_sems.at[1, k], (q, r),
            )
        )
    for copy in mids + cots + rights:
        copy.start()
    local[0].wait()
    for copy in mids:
        copy.wait_recv()
    along = []
    for k in range(1, chips):
        peer = lax.rem(r + 2 * k, rows)
        along.append(remote(left_mid, left_all.at[r], row_sems.at[0, k], row_sems.at[1, k], (g, peer)))
    pairs = [remote(left_mid, left_all.at[r], pair_sems.at[0, 0], pair_sems.at[1, 0], (g, sibling))]
    keep = pltpu.make_async_copy(left_mid, left_all.at[r], own.at[3])
    for copy in along + pairs + [keep]:
        copy.start()
    local[1].wait()
    for copy in cots:
        copy.wait_recv()
    cot_rows = []
    for k in range(1, rows):
        peer = lax.rem(r + k, rows)
        cot_rows.append(
            remote(cot_mid.at[:, peer], cot_all.at[r], cot_row_sems.at[0, k], cot_row_sems.at[1, k], (g, peer))
        )
    keep_cot = pltpu.make_async_copy(cot_mid.at[:, r], cot_all.at[r], own.at[4])
    for copy in cot_rows + [keep_cot]:
        copy.start()
    for k in range(1, chips):
        along[k - 1].wait_recv()
        source = lax.rem(r + rows - 2 * k, rows)
        pairs.append(
            remote(
                left_all.at[source], left_all.at[source],
                pair_sems.at[0, k], pair_sems.at[1, k], (g, sibling),
            )
        )
        pairs[-1].start()
    for copy in pairs + cot_rows + rights:
        copy.wait_recv()
    for copy in mids + cots + rights + along + pairs + cot_rows:
        copy.wait_send()
    local[2].wait()
    keep.wait()
    keep_cot.wait()


def collect(
    copies, rows, share,
    back, part, right_out, left_out,
    mine, pair_in, total, chip_in, done, own, back_sems, pair_sems, row_sems, out_sems,
):
    g, r, core, sibling = place(copies, rows)
    chips = rows // 2
    chip = r // 2
    greet(
        g, r,
        [(lax.rem(g + k, copies), r) for k in range(1, copies)]
        + [(g, lax.rem(r + 2 * k, rows)) for k in range(1, chips)]
        + [(g, sibling)],
    )
    pairs, loads = [], []
    for z in range(chips):
        pairs.append(
            remote(part.at[2 * z + 1 - core], pair_in.at[z], pair_sems.at[0, z], pair_sems.at[1, z], (g, sibling))
        )
        loads.append(pltpu.make_async_copy(part.at[2 * z + core], mine.at[z], own.at[z]))
    backs = []
    for k in range(1, copies):
        q = lax.rem(g + k, copies)
        backs.append(
            remote(
                back.at[:, q], right_out.at[pl.ds(g * share, share)],
                back_sems.at[0, k], back_sems.at[1, k], (q, r),
            )
        )
    keep = pltpu.make_async_copy(back.at[:, g], right_out.at[pl.ds(g * share, share)], own.at[chips])
    for copy in pairs + loads + backs + [keep]:
        copy.start()
    for z in range(chips):
        pairs[z].wait_recv()
        loads[z].wait()
    rights = []
    for k in range(1, chips):
        z = lax.rem(chip + k, chips)
        total[z] = (mine[z].astype(jnp.float32) + pair_in[z].astype(jnp.float32)).astype(total.dtype)
        rights.append(
            remote(total.at[z], chip_in.at[k], row_sems.at[0, k], row_sems.at[1, k], (g, 2 * z + core))
        )
        rights[-1].start()
    for copy in rights:
        copy.wait_recv()
    rest = mine[chip].astype(jnp.float32) + pair_in[chip].astype(jnp.float32)
    for k in range(1, chips):
        rest = rest + chip_in[k].astype(jnp.float32)
    done[...] = rest.astype(done.dtype).reshape(done.shape)
    lefts = []
    for k in range(1, copies):
        q = lax.rem(g + k, copies)
        lefts.append(remote(done.at[q], left_out.at[:, g], out_sems.at[0, k], out_sems.at[1, k], (q, r)))
    keep_left = pltpu.make_async_copy(done.at[g], left_out.at[:, g], own.at[chips + 1])
    for copy in lefts + [keep_left]:
        copy.start()
    for copy in backs + lefts:
        copy.wait_recv()
    for copy in pairs + backs + rights + lefts:
        copy.wait_send()
    keep.wait()
    keep_left.wait()


def sems(*shape):
    return pltpu.SemaphoreType.DMA(shape)


def on_device(left_proj, left_gate, right_factor, cotangent, residue_mask):
    copies = lax.axis_size("copy")
    rows = lax.axis_size("row")
    row_here = lax.axis_index("row")
    channels, held, length = left_proj.shape
    share = channels // copies
    block = right_factor.shape[1]
    bf16 = jnp.bfloat16
    keep_rows = lax.dynamic_slice_in_dim(residue_mask, row_here * held, held).astype(jnp.float32)
    keep_cols = residue_mask.astype(jnp.float32)
    keep_both = keep_rows[None, :, None] * keep_cols[None, None, :]
    opened = jax.nn.sigmoid(left_gate.astype(jnp.float32))
    left_factor = (keep_both * opened * left_proj.astype(jnp.float32)).astype(bf16)
    left_in = left_factor.transpose(1, 0, 2).reshape(held, copies, share, length)

    size = held * share * block
    tall = -(-size // 2048) * 16
    cot = cotangent.reshape(copies, share, held, rows, block).transpose(0, 3, 2, 1, 4)
    cot = jnp.pad(cot.reshape(copies, rows, size), ((0, 0), (0, 0), (0, tall * 128 - size)))
    cot = cot.reshape(copies, rows, tall, 128)

    def kernel(body):
        return lambda *refs: body(copies, rows, share, *refs)

    chips = rows // 2
    right, left, cot = pl.pallas_call(
        kernel(spread),
        out_shape=(
            jax.ShapeDtypeStruct((share, copies, block, length), bf16),
            jax.ShapeDtypeStruct((rows, copies, held, share, length), bf16),
            jax.ShapeDtypeStruct((rows, copies, tall, 128), bf16),
        ),
        in_specs=[ANY] * 3,
        out_specs=(ANY,) * 3,
        scratch_shapes=[
            pltpu.VMEM((copies, held, share, length), bf16),
            pltpu.VMEM((copies, rows, tall, 128), bf16),
            sems(5),
            sems(2, copies),
            sems(2, copies),
            sems(2, copies),
            sems(2, chips),
            sems(2, chips),
            sems(2, rows),
        ],
        compiler_params=pltpu.CompilerParams(
            collective_id=0, has_side_effects=True, vmem_limit_bytes=48 << 20
        ),
    )(right_factor, left_in, cot)

    cot = cot.reshape(rows, copies, tall * 128)[:, :, :size].reshape(rows, copies, held, share, block)
    cot = cot.transpose(3, 0, 1, 2, 4)
    matrix = jnp.concatenate(
        [
            jnp.roll(cot, source, axis=2).reshape(share, rows * copies * held, block)
            for source in range(copies)
        ],
        axis=2,
    )
    left = left.reshape(rows * copies * held, share, length).transpose(1, 0, 2)
    back = jnp.einsum("cij,cik->cjk", matrix, left, preferred_element_type=jnp.float32).astype(bf16)
    back = back.reshape(share, copies, block, length)
    right = right.reshape(share, copies * block, length)
    part = jnp.einsum("cij,cjk->cik", matrix, right, preferred_element_type=jnp.float32).astype(bf16)
    part = part.transpose(1, 0, 2).reshape(rows, copies * held, share, length)

    slab = (copies * held, share, length)
    grad_right, left_sum = pl.pallas_call(
        kernel(collect),
        out_shape=(
            jax.ShapeDtypeStruct(right_factor.shape, bf16),
            jax.ShapeDtypeStruct((held, copies, share, length), bf16),
        ),
        in_specs=[ANY] * 2,
        out_specs=(ANY,) * 2,
        scratch_shapes=[
            pltpu.VMEM((chips,) + slab, bf16),
            pltpu.VMEM((chips,) + slab, bf16),
            pltpu.VMEM((chips,) + slab, bf16),
            pltpu.VMEM((chips,) + slab, bf16),
            pltpu.VMEM((copies, held, share, length), bf16),
            sems(chips + 2),
            sems(2, copies),
            sems(2, chips),
            sems(2, chips),
            sems(2, copies),
        ],
        compiler_params=pltpu.CompilerParams(
            collective_id=1, has_side_effects=True, vmem_limit_bytes=48 << 20
        ),
    )(back, part)

    left_wide = left_sum.reshape(held, channels, length).transpose(1, 0, 2).astype(jnp.float32)
    grad_proj = (left_wide * keep_both * opened).astype(bf16)
    grad_gate = (
        left_wide * keep_both * left_proj.astype(jnp.float32) * opened * (1.0 - opened)
    ).astype(bf16)
    return (grad_proj, grad_gate, grad_right)


def solution(mesh):
    spec = P(None, "row", "copy")
    return jax.shard_map(
        on_device,
        mesh=mesh,
        in_specs=(spec, spec, spec, spec, P()),
        out_specs=(spec, spec, spec),
        check_vma=False,
    )
```

time: 567 us -> 167 us (0.29)
  waiting for transfers between devices: 326 us -> 0 us
  blocking collectives: 160 us -> 0 us
  Pallas kernels: 0 us -> 131 us
  matrix products: 37.1 us -> 10.9 us
  between operations: 14.1 us -> 0.86 us
  starting transfers between devices: 9.33 us -> 0 us
    all_gather x3 -> x0, waiting for transfers between devices: 207 us -> none  [the longest x1 175 us: on_device(): lax.all_gather(right_local[None], 'copy', axis=0, tiled=True)]
    all_to_all x3 -> x0, blocking collectives: 160 us -> none  [the longest x1 110 us: on_device(): lax.all_to_all(right_totals.astype(jnp.bfloat16), 'row', split_axis=1, co...]
    pallas_call x0 -> x2, Pallas kernels: none -> 131 us  [the longest x1 70.1 us: on_device(): pl.pallas_call(kernel(spread), out_shape=(jax.ShapeDtypeStruct((share, co...]
    all_to_all x2 -> x0, waiting for transfers between devices: 119 us -> none  [the longest x1 104 us: on_device(): lax.all_to_all(right_factor, 'row', split_axis=0, concat_axis=1, tiled=True)]
    dot_general x8 -> x2, matrix products: 37.1 us -> 10.9 us  [the longest x1 7.94 us: on_device(): jnp.einsum('cij,cik->cjk', matrix, left, preferred_element_type=jnp.float32)]
    all_to_all x2 -> x0, starting transfers between devices: 9.21 us -> none  [the longest x1 4.61 us: on_device(): lax.all_to_all(right_factor, 'row', split_axis=0, concat_axis=1, tiled=True)]
    all_to_all x4 -> x0, local copies, waits for them, and re-layouts: 8.64 us -> none  [the longest x1 5.25 us: on_device(): lax.all_to_all(right_factor, 'row', split_axis=0, concat_axis=1, tiled=True)]
    reshape x0 -> x8, local copies, waits for them, and re-layouts: none -> 8.24 us  [the longest x1 2.6 us: on_device(): cot.reshape(copies, rows, size)]
  transfers between devices with their start and end apart: 5 -> 0, of which waited for: 4 -> 0; matrix products, arithmetic and copies ran while one was open for 1% -> 0% of each run, Pallas kernels for 0% -> 0%
where the time goes in v1:
time: 167 us; the launch traced here: 166 us
  Pallas kernels  131 us (78%)
  local copies, waits for them, and re-layouts  18.4 us (11%)
  matrix products  10.9 us (7%)
  other arithmetic  5.21 us (3%)
    pallas_call x1, Pallas kernels, on_device(): pl.pallas_call(kernel(spread), out_shape=(jax.ShapeDtypeStruct((share, co...  70.1 us
    pallas_call x1, Pallas kernels, on_device(): pl.pallas_call(kernel(collect), out_shape=(jax.ShapeDtypeStruct(right_fac...  60.9 us
    dot_general x1, matrix products, on_device(): jnp.einsum('cij,cik->cjk', matrix, left, preferred_element_type=jnp.float32)  7.94 us
    unnamed x15, local copies, waits for them, and re-layouts  7.75 us

profile of v1, /device:TPU:0, one launch (start us, length us, event | category | flops | bytes accessed | tf_op | source)
XLA Modules:
  0.0 166.4 jit_solution(16635232146828502995)
XLA Ops:
  0.6 0.8 dynamic-slice_convert_fusion
  1.4 0.7 convert_element_type.42
  2.1 0.1 broadcast_multiply_fusion
  2.2 1.5 fusion.6
  3.6 2.2 %reshape.84 = bf16[4,32,5,8,48]{4,3,1,0,2:T(8,128)(2,1)S(1)} reshape(bf16[128,5,384]{2,0,1:T(8,128)(2,1)} %param.8) | data formatting | bytes 983040 | tf_op jit(solution)/shard_map/reshape | solution.py:190
  5.8 0.3 copy.12
  6.1 2.6 %reshape.85 = bf16[4,8,7680]{2,1,0:T(8,128)(2,1)S(1)} reshape(bf16[4,8,5,32,48]{4,3,2,1,0:T(8,128)(2,1)S(1)} %copy.12) | data formatting | bytes 983040 | tf_op jit(solution)/shard_map/reshape | solution.py:191
  8.7 0.1 copy.27
  8.9 70.1 %shard_map.76 = (bf16[32,4,48,384]{3,2,1,0:T(8,128)(2,1)}, bf16[8,4,5,32,384]{4,3,2,1,0:T(8,128)(2,1)S(1)}, bf16[8,4,64,128]{3,2,1,0:T(8,128)(2,1)S(1)}) custom-call(bf16[128,48,384]{2,1,0:T(8,128)(2,1)} %refs_0_.1, bf16[5,4,32,384]{3,2,1,0:T(8,128)(2,1)S(1)} %bitcast.48, bf16[4,8,64,128]{3,2,1,0:T(8,128)(2,1)S(1)} %copy.27), custom_call_target="tpu_custom_call" | custom-call | tf_op jit(solution)/shard_map/pallas_call | solution.py:198
  79.0 0.0 copy-start
  79.0 1.9 %copy-done = bf16[8,4,5,32,384]{4,3,2,1,0:T(8,128)(2,1)} copy-done((bf16[8,4,5,32,384]{4,3,2,1,0:T(8,128)(2,1)}, bf16[8,4,5,32,384]{4,3,2,1,0:T(8,128)(2,1)S(1)}, u32[]{:S(2)}) %copy-start) | copy-done | bytes 3932184
  80.9 0.1 reshape.87
  81.0 0.2 slice.34
  81.2 1.3 reshape.88
  82.6 0.5 copy.13
  83.1 0.2 fusion.15
  83.3 0.3 pad_maximum_fusion.2
  83.6 0.5 copy.15
  84.1 0.0 slice-start
  84.1 0.3 fusion.14
  84.4 0.0 slice-start.1
  84.4 0.5 pad_maximum_fusion.1
  84.9 0.5 copy.14
  85.5 0.5 copy.16
  86.0 0.0 slice-done
  86.0 0.7 slice-done.1
  86.6 0.0 copy-start.1
  86.6 2.9 %convert_bitcast_fusion = bf16[160,32,384]{2,0,1:T(8,128)(2,1)S(1)} fusion(bf16[32,192,384]{2,1,0:T(8,128)(2,1)S(1)} %bitcast.61, bf16[32,160,48]{2,1,0:T(8,128)(2,1)S(1)} %copy.16, bf16[32,160,48]{2,1,0:T(8,128)(2,1)S(1)} %copy.15, bf16[32,160,48]{2,1,0:T(8,128)(2,1)S(1)} %copy.14, bf16[32,160,48]{2,1,0:T(8,128)(2,1)S(1)} %copy.13), kind=kOutput, calls=%fused_computation.3 | convolution fusion | flops 764805120 | bytes 10616832 | tf_op jit(solution)/shard_map/cij,cjk->cik/dot_general | solution.py:236
  89.6 0.0 copy-done.1
  89.6 7.9 %fusion.3 = bf16[32,192,384]{2,1,0:T(8,128)(2,1)} fusion(bf16[160,32,384]{2,1,0:T(8,128)(2,1)S(1)} %bitcast.49, bf16[32,160,48]{2,1,0:T(8,128)(2,1)S(1)} %copy.16, bf16[32,160,48]{2,1,0:T(8,128)(2,1)S(1)} %copy.15, bf16[32,160,48]{2,1,0:T(8,128)(2,1)S(1)} %copy.14, bf16[32,160,48]{2,1,0:T(8,128)(2,1)S(1)} %copy.13), kind=kOutput, calls=%fused_computation.4 | convolution fusion | flops 765198336 | bytes 10616832 | tf_op jit(solution)/shard_map/cij,cik->cjk/dot_general | solution.py:233
  97.5 1.4 copy.18
  98.9 0.0 copy-start.2
  99.0 0.0 copy-start.3
  99.0 60.9 %shard_map.77 = (bf16[128,48,384]{2,1,0:T(8,128)(2,1)}, bf16[5,4,32,384]{3,2,1,0:T(8,128)(2,1)S(1)}) custom-call(bf16[32,4,48,384]{3,2,1,0:T(8,128)(2,1)} %bitcast.58, bf16[8,20,32,384]{3,2,1,0:T(8,128)(2,1)S(1)} %bitcast.47), custom_call_target="tpu_custom_call" | custom-call | tf_op jit(solution)/shard_map/pallas_call | solution.py:240
  159.9 0.0 copy-done.2
  159.9 0.0 copy-done.3
  159.9 1.5 fusion.9
  161.4 5.0 %copy.29 = bf16[128,48,384]{2,1,0:T(8,128)(2,1)} copy(bf16[128,48,384]{2,1,0:T(8,128)(2,1)} %get-tuple-element.28) | data formatting | bytes 9437184
  (3 shorter events, 0.1 us)
Async XLA Ops:
  79.0 1.9 %copy-start = (bf16[8,4,5,32,384]{4,3,2,1,0:T(8,128)(2,1)}, bf16[8,4,5,32,384]{4,3,2,1,0:T(8,128)(2,1)S(1)}, u32[]{:S(2)}) copy-start(bf16[8,4,5,32,384]{4,3,2,1,0:T(8,128)(2,1)S(1)} %get-tuple-element.9) | copy-start | bytes 11796484
  84.1 1.9 %slice-start = ((s8[4718592]{0:T(1024)(128)(4,1)}), s8[524288]{0:T(1024)(128)(4,1)S(1)}, s32[]{:S(2)}) async-start(s8[4718592]{0:T(1024)(128)(4,1)} %bitcast.59), calls=%async_computation | async-start | bytes 1048576
  84.4 2.2 %slice-start.1 = ((s8[4718592]{0:T(1024)(128)(4,1)}), s8[4194304]{0:T(1024)(128)(4,1)S(1)}, s32[]{:S(2)}) async-start(s8[4718592]{0:T(1024)(128)(4,1)} %bitcast.59), calls=%async_computation.1 | async-start | bytes 8388608
  86.6 2.9 %copy-start.1 = (bf16[8,4,5,32,384]{4,3,2,1,0:T(8,128)(2,1)S(1)}, bf16[8,4,5,32,384]{4,3,2,1,0:T(8,128)(2,1)}, u32[]{:S(2)}) copy-start(bf16[8,4,5,32,384]{4,3,2,1,0:T(8,128)(2,1)} %copy-done) | copy-start | bytes 11796484
  98.9 61.0 %copy-start.2 = (bf16[128,5,384]{2,0,1:T(8,128)(2,1)S(1)}, bf16[128,5,384]{2,0,1:T(8,128)(2,1)}, u32[]{:S(2)}) copy-start(bf16[128,5,384]{2,0,1:T(8,128)(2,1)} %param.5) | copy-start | bytes 1474564
  99.0 61.0 %copy-start.3 = (bf16[128,5,384]{2,0,1:T(8,128)(2,1)S(1)}, bf16[128,5,384]{2,0,1:T(8,128)(2,1)}, u32[]{:S(2)}) copy-start(bf16[128,5,384]{2,0,1:T(8,128)(2,1)} %param.6) | copy-start | bytes 1474564

commit v2 on v1

--- a/solution.py
+++ b/solution.py
@@ -104,24 +104,25 @@
 
 def collect(
     copies, rows, share,
-    back, part, right_out, left_out,
-    mine, pair_in, total, chip_in, done, own, back_sems, pair_sems, row_sems, out_sems,
+    back, matrix, right, right_out, left_out,
+    factor, held_matrix, part, pair_in, chip_in, done,
+    own, back_sems, pair_sems, row_sems, out_sems,
 ):
     g, r, core, sibling = place(copies, rows)
     chips = rows // 2
     chip = r // 2
+    loads = [
+        pltpu.make_async_copy(matrix, held_matrix, own.at[0]),
+        pltpu.make_async_copy(right, factor, own.at[1]),
+    ]
+    for copy in loads:
+        copy.start()
     greet(
         g, r,
         [(lax.rem(g + k, copies), r) for k in range(1, copies)]
         + [(g, lax.rem(r + 2 * k, rows)) for k in range(1, chips)]
         + [(g, sibling)],
     )
-    pairs, loads = [], []
-    for z in range(chips):
-        pairs.append(
-            remote(part.at[2 * z + 1 - core], pair_in.at[z], pair_sems.at[0, z], pair_sems.at[1, z], (g, sibling))
-        )
-        loads.append(pltpu.make_async_copy(part.at[2 * z + core], mine.at[z], own.at[z]))
     backs = []
     for k in range(1, copies):
         q = lax.rem(g + k, copies)
@@ -131,23 +132,51 @@
                 back_sems.at[0, k], back_sems.at[1, k], (q, r),
             )
         )
-    keep = pltpu.make_async_copy(back.at[:, g], right_out.at[pl.ds(g * share, share)], own.at[chips])
-    for copy in pairs + loads + backs + [keep]:
-        copy.start()
-    for z in range(chips):
-        pairs[z].wait_recv()
-        loads[z].wait()
+    keep = pltpu.make_async_copy(back.at[:, g], right_out.at[pl.ds(g * share, share)], own.at[2])
+    for copy in backs + [keep]:
+        copy.start()
+    for copy in loads:
+        copy.wait()
+    step = 16 if share % 16 == 0 else share
+    groups, tall = held_matrix.shape[1], held_matrix.shape[2]
+    slab = part.shape[1:]
+
+    def multiply(group, carry):
+        for first in range(0, share, step):
+            product = lax.dot_general(
+                held_matrix[first : first + step, group],
+                factor[first : first + step],
+                (((2,), (1,)), ((0,), (0,))),
+                preferred_element_type=jnp.float32,
+            )
+            turned = jnp.swapaxes(product.astype(part.dtype), 0, 1)
+            part[pl.ds(group * (rows // groups), rows // groups), :, first : first + step, :] = (
+                turned.reshape(rows // groups, slab[0], step, slab[2])
+            )
+        return carry
+
+    lax.fori_loop(0, groups, multiply, 0)
+    pairs = []
+    for k in range(chips):
+        z = lax.rem(chip + 1 + k, chips)
+        pairs.append(
+            remote(part.at[2 * z + 1 - core], pair_in.at[k], pair_sems.at[0, k], pair_sems.at[1, k], (g, sibling))
+        )
+        pairs[-1].start()
     rights = []
     for k in range(1, chips):
         z = lax.rem(chip + k, chips)
-        total[z] = (mine[z].astype(jnp.float32) + pair_in[z].astype(jnp.float32)).astype(total.dtype)
+        pairs[k - 1].wait_recv()
+        mine = part[2 * z + core].astype(jnp.float32) + pair_in[k - 1].astype(jnp.float32)
+        part[2 * z + core] = mine.astype(part.dtype)
         rights.append(
-            remote(total.at[z], chip_in.at[k], row_sems.at[0, k], row_sems.at[1, k], (g, 2 * z + core))
+            remote(part.at[2 * z + core], chip_in.at[k], row_sems.at[0, k], row_sems.at[1, k], (g, 2 * z + core))
         )
         rights[-1].start()
+    pairs[chips - 1].wait_recv()
     for copy in rights:
         copy.wait_recv()
-    rest = mine[chip].astype(jnp.float32) + pair_in[chip].astype(jnp.float32)
+    rest = part[r].astype(jnp.float32) + pair_in[chips - 1].astype(jnp.float32)
     for k in range(1, chips):
         rest = rest + chip_in[k].astype(jnp.float32)
     done[...] = rest.astype(done.dtype).reshape(done.shape)
@@ -155,7 +184,7 @@
     for k in range(1, copies):
         q = lax.rem(g + k, copies)
         lefts.append(remote(done.at[q], left_out.at[:, g], out_sems.at[0, k], out_sems.at[1, k], (q, r)))
-    keep_left = pltpu.make_async_copy(done.at[g], left_out.at[:, g], own.at[chips + 1])
+    keep_left = pltpu.make_async_copy(done.at[g], left_out.at[:, g], own.at[3])
     for copy in lefts + [keep_left]:
         copy.start()
     for copy in backs + lefts:
@@ -216,7 +245,7 @@
             sems(2, rows),
         ],
         compiler_params=pltpu.CompilerParams(
-            collective_id=0, has_side_effects=True, vmem_limit_bytes=48 << 20
+            collective_id=0, has_side_effects=True, vmem_limit_bytes=8 << 20
         ),
     )(right_factor, left_in, cot)
 
@@ -233,34 +262,37 @@
     back = jnp.einsum("cij,cik->cjk", matrix, left, preferred_element_type=jnp.float32).astype(bf16)
     back = back.reshape(share, copies, block, length)
     right = right.reshape(share, copies * block, length)
-    part = jnp.einsum("cij,cjk->cik", matrix, right, preferred_element_type=jnp.float32).astype(bf16)
-    part = part.transpose(1, 0, 2).reshape(rows, copies * held, share, length)
+    groups = rows // 8 if rows % 8 == 0 else 1
+    grouped = matrix.reshape(share, groups, matrix.shape[1] // groups, copies * block)
 
     slab = (copies * held, share, length)
+    slab_bytes = 2 * copies * held * share * length
     grad_right, left_sum = pl.pallas_call(
         kernel(collect),
         out_shape=(
             jax.ShapeDtypeStruct(right_factor.shape, bf16),
             jax.ShapeDtypeStruct((held, copies, share, length), bf16),
         ),
-        in_specs=[ANY] * 2,
+        in_specs=[ANY] * 3,
         out_specs=(ANY,) * 2,
         scratch_shapes=[
-            pltpu.VMEM((chips,) + slab, bf16),
-            pltpu.VMEM((chips,) + slab, bf16),
+            pltpu.VMEM(right.shape, bf16),
+            pltpu.VMEM(grouped.shape, bf16),
+            pltpu.VMEM((rows,) + slab, bf16),
             pltpu.VMEM((chips,) + slab, bf16),
             pltpu.VMEM((chips,) + slab, bf16),
             pltpu.VMEM((copies, held, share, length), bf16),
-            sems(chips + 2),
+            sems(4),
             sems(2, copies),
             sems(2, chips),
             sems(2, chips),
             sems(2, copies),
         ],
         compiler_params=pltpu.CompilerParams(
-            collective_id=1, has_side_effects=True, vmem_limit_bytes=48 << 20
+            collective_id=1, has_side_effects=True,
+            vmem_limit_bytes=(24 << 20) + 2 * rows * slab_bytes,
         ),
-    )(back, part)
+    )(back, grouped, right)
 
     left_wide = left_sum.reshape(held, channels, length).transpose(1, 0, 2).astype(jnp.float32)
     grad_proj = (left_wide * keep_both * opened).astype(bf16)

time: 167 us -> 166 us (level)
  matrix products: 10.9 us -> 6.34 us
  other arithmetic: 5.21 us -> 7.76 us
  local copies, waits for them, and re-layouts: 18.4 us -> 20.7 us
    dot_general x1 -> x0, matrix products: 2.92 us -> none  [on_device(): jnp.einsum('cij,cjk->cik', matrix, right, preferred_element_type=jnp.floa...]
    reshape x0 -> x1, other arithmetic: none -> 2.55 us  [on_device(): matrix.reshape(share, groups, matrix.shape[1] // groups, copies * block)]
    unnamed x15 -> x20, local copies, waits for them, and re-layouts: 7.75 us -> 10.1 us
where the time goes in v2:
time: 166 us
  Pallas kernels  130 us (78%)
  local copies, waits for them, and re-layouts  20.7 us (12%)
  other arithmetic  7.76 us (5%)
  matrix products  6.34 us (4%)
    pallas_call x1, Pallas kernels, on_device(): pl.pallas_call(kernel(spread), out_shape=(jax.ShapeDtypeStruct((share, co...  70 us
    pallas_call x1, Pallas kernels, on_device(): pl.pallas_call(kernel(collect), out_shape=(jax.ShapeDtypeStruct(right_fac...  60 us
    unnamed x20, local copies, waits for them, and re-layouts  10.1 us
    dot_general x1, matrix products, on_device(): jnp.einsum('cij,cik->cjk', matrix, left, preferred_element_type=jnp.float32)  6.34 us

profile of v2, /device:TPU:0, one launch (start us, length us, event | category | flops | bytes accessed | tf_op | source)
XLA Modules:
  0.0 165.7 jit_solution(14268306105809926191)
XLA Ops:
  0.6 0.8 dynamic-slice_convert_fusion
  1.4 0.7 convert_element_type.35
  2.1 0.1 broadcast_multiply_fusion
  2.2 1.5 fusion.6
  3.6 2.2 %reshape.84 = bf16[4,32,5,8,48]{4,3,1,0,2:T(8,128)(2,1)S(1)} reshape(bf16[128,5,384]{2,0,1:T(8,128)(2,1)} %param.8) | data formatting | bytes 983040 | tf_op jit(solution)/shard_map/reshape | solution.py:219
  5.8 0.3 copy.10
  6.1 2.6 %reshape.85 = bf16[4,8,7680]{2,1,0:T(8,128)(2,1)S(1)} reshape(bf16[4,8,5,32,48]{4,3,2,1,0:T(8,128)(2,1)S(1)} %copy.10) | data formatting | bytes 983040 | tf_op jit(solution)/shard_map/reshape | solution.py:220
  8.7 0.1 copy.30
  8.9 0.0 copy-start
  8.9 2.3 %copy-done = bf16[128,48,384]{2,1,0:T(8,128)(2,1)S(1)} copy-done((bf16[128,48,384]{2,1,0:T(8,128)(2,1)S(1)}, bf16[128,48,384]{2,1,0:T(8,128)(2,1)}, u32[]{:S(2)}) %copy-start) | copy-done | bytes 4718616
  11.2 70.0 %shard_map.76 = (bf16[32,4,48,384]{3,2,1,0:T(8,128)(2,1)S(1)}, bf16[8,4,5,32,384]{4,3,2,1,0:T(8,128)(2,1)S(1)}, bf16[8,4,64,128]{3,2,1,0:T(8,128)(2,1)S(1)}) custom-call(bf16[128,48,384]{2,1,0:T(8,128)(2,1)S(1)} %copy-done, bf16[5,4,32,384]{3,2,1,0:T(8,128)(2,1)S(1)} %bitcast.50, bf16[4,8,64,128]{3,2,1,0:T(8,128)(2,1)S(1)} %copy.30), custom_call_target="tpu_custom_call" | custom-call | tf_op jit(solution)/shard_map/pallas_call | solution.py:227
  81.2 0.0 copy-start.1
  81.2 2.2 %copy-done.1 = bf16[32,4,48,384]{3,2,1,0:T(8,128)(2,1)} copy-done((bf16[32,4,48,384]{3,2,1,0:T(8,128)(2,1)}, bf16[32,4,48,384]{3,2,1,0:T(8,128)(2,1)S(1)}, u32[]{:S(2)}) %copy-start.1) | copy-done | bytes 4718616
  83.4 0.0 copy-start.2
  83.4 1.9 %copy-done.2 = bf16[8,4,5,32,384]{4,3,2,1,0:T(8,128)(2,1)} copy-done((bf16[8,4,5,32,384]{4,3,2,1,0:T(8,128)(2,1)}, bf16[8,4,5,32,384]{4,3,2,1,0:T(8,128)(2,1)S(1)}, u32[]{:S(2)}) %copy-start.2) | copy-done | bytes 3932184
  85.2 0.1 reshape.87
  85.4 0.2 slice.34
  85.6 0.1 copy.21
  85.7 1.3 reshape.88
  87.0 0.3 copy.12
  87.3 0.5 copy.16
  87.8 0.3 fusion.16
  88.1 0.3 pad_maximum_fusion.2
  88.4 0.3 copy.14
  88.7 0.5 copy.18
  89.2 0.4 fusion.15
  89.6 0.5 pad_maximum_fusion.1
  90.1 0.3 copy.13
  90.4 0.5 copy.17
  91.0 0.0 copy-start.3
  91.0 0.3 copy.15
  91.2 0.0 slice-start
  91.3 0.5 copy.19
  91.8 1.3 copy-done.3
  93.1 0.0 slice-start.1
  93.1 6.3 %fusion.3 = bf16[32,192,384]{2,1,0:T(8,128)(2,1)S(1)} fusion(bf16[160,32,384]{2,1,0:T(8,128)(2,1)S(1)} %bitcast.51, bf16[32,160,48]{2,1,0:T(8,128)(2,1)S(1)} %copy.19, bf16[32,160,48]{2,1,0:T(8,128)(2,1)S(1)} %copy.18, bf16[32,160,48]{2,1,0:T(8,128)(2,1)S(1)} %copy.17, bf16[32,160,48]{2,1,0:T(8,128)(2,1)S(1)} %copy.16), kind=kOutput, calls=%fused_computation.3 | convolution fusion | flops 765198336 | bytes 10616832 | tf_op jit(solution)/shard_map/cij,cik->cjk/dot_general | solution.py:262
  99.4 2.5 %fusion.13.refs_1_ = bf16[32,1,160,192]{3,2,1,0:T(8,128)(2,1)S(1)} fusion(bf16[32,160,48]{2,1,0:T(8,128)(2,1)S(1)} %copy.19, bf16[32,160,48]{2,1,0:T(8,128)(2,1)S(1)} %copy.18, bf16[32,160,48]{2,1,0:T(8,128)(2,1)S(1)} %copy.17, bf16[32,160,48]{2,1,0:T(8,128)(2,1)S(1)} %copy.16), kind=kLoop, calls=%fused_computation.23 | loop fusion | flops 7864320 | bytes 3932160 | tf_op jit(solution)/shard_map/reshape | solution.py:266
  102.0 0.0 slice-done
  102.0 0.0 slice-done.1
  102.0 0.0 copy-start.4
  102.0 0.0 copy-start.5
  102.0 60.0 %shard_map.77 = (bf16[128,48,384]{2,1,0:T(8,128)(2,1)S(1)}, bf16[5,4,32,384]{3,2,1,0:T(8,128)(2,1)S(1)}) custom-call(bf16[32,4,48,384]{3,2,1,0:T(8,128)(2,1)S(1)} %bitcast.49, bf16[32,1,160,192]{3,2,1,0:T(8,128)(2,1)S(1)} %fusion.13.refs_1_, bf16[32,192,384]{2,1,0:T(8,128)(2,1)S(1)} %bitcast.48), custom_call_target="tpu_custom_call" | custom-call | tf_op jit(solution)/shard_map/pallas_call | solution.py:270
  162.0 0.0 copy-done.4
  162.0 0.0 copy-done.5
  162.0 1.5 fusion.9
  163.5 2.2 %copy.32 = bf16[128,48,384]{2,1,0:T(8,128)(2,1)} copy(bf16[128,48,384]{2,1,0:T(8,128)(2,1)S(1)} %get-tuple-element.28) | data formatting | bytes 9437184
  (3 shorter events, 0.1 us)
Async XLA Ops:
  8.9 2.3 %copy-start = (bf16[128,48,384]{2,1,0:T(8,128)(2,1)S(1)}, bf16[128,48,384]{2,1,0:T(8,128)(2,1)}, u32[]{:S(2)}) copy-start(bf16[128,48,384]{2,1,0:T(8,128)(2,1)} %refs_0_.1) | copy-start | bytes 14155780
  81.2 2.2 %copy-start.1 = (bf16[32,4,48,384]{3,2,1,0:T(8,128)(2,1)}, bf16[32,4,48,384]{3,2,1,0:T(8,128)(2,1)S(1)}, u32[]{:S(2)}) copy-start(bf16[32,4,48,384]{3,2,1,0:T(8,128)(2,1)S(1)} %get-tuple-element.10) | copy-start | bytes 14155780
  83.4 1.9 %copy-start.2 = (bf16[8,4,5,32,384]{4,3,2,1,0:T(8,128)(2,1)}, bf16[8,4,5,32,384]{4,3,2,1,0:T(8,128)(2,1)S(1)}, u32[]{:S(2)}) copy-start(bf16[8,4,5,32,384]{4,3,2,1,0:T(8,128)(2,1)S(1)} %get-tuple-element.9) | copy-start | bytes 11796484
  91.0 2.1 %copy-start.3 = (bf16[8,4,5,32,384]{4,3,2,1,0:T(8,128)(2,1)S(1)}, bf16[8,4,5,32,384]{4,3,2,1,0:T(8,128)(2,1)}, u32[]{:S(2)}) copy-start(bf16[8,4,5,32,384]{4,3,2,1,0:T(8,128)(2,1)} %copy-done.2) | copy-start | bytes 11796484
  91.2 10.7 %slice-start = ((s8[4718592]{0:T(1024)(128)(4,1)}), s8[4194304]{0:T(1024)(128)(4,1)S(1)}, s32[]{:S(2)}) async-start(s8[4718592]{0:T(1024)(128)(4,1)} %bitcast.46), calls=%async_computation | async-start | bytes 8388608
  93.1 8.9 %slice-start.1 = ((s8[4718592]{0:T(1024)(128)(4,1)}), s8[524288]{0:T(1024)(128)(4,1)S(1)}, s32[]{:S(2)}) async-start(s8[4718592]{0:T(1024)(128)(4,1)} %bitcast.46), calls=%async_computation.1 | async-start | bytes 1048576
  102.0 60.0 %copy-start.4 = (bf16[128,5,384]{2,0,1:T(8,128)(2,1)S(1)}, bf16[128,5,384]{2,0,1:T(8,128)(2,1)}, u32[]{:S(2)}) copy-start(bf16[128,5,384]{2,0,1:T(8,128)(2,1)} %param.5) | copy-start | bytes 1474564
  102.0 60.0 %copy-start.5 = (bf16[128,5,384]{2,0,1:T(8,128)(2,1)S(1)}, bf16[128,5,384]{2,0,1:T(8,128)(2,1)}, u32[]{:S(2)}) copy-start(bf16[128,5,384]{2,0,1:T(8,128)(2,1)} %param.6) | copy-start | bytes 1474564

commit v3 on v2

--- a/solution.py
+++ b/solution.py
@@ -30,8 +30,8 @@
 
 def spread(
     copies, rows, share,
-    right, left, cot, right_all, left_all, cot_all,
-    left_mid, cot_mid, own, mid_sems, cot_sems, right_sems, row_sems, pair_sems, cot_row_sems,
+    left, cot, left_all, cot_all,
+    left_mid, cot_mid, own, mid_sems, cot_sems, row_sems, pair_sems, cot_row_sems,
 ):
     g, r, core, sibling = place(copies, rows)
     chips = rows // 2
@@ -43,22 +43,15 @@
     local = [
         pltpu.make_async_copy(left.at[:, g], left_mid.at[g], own.at[0]),
         pltpu.make_async_copy(cot.at[g], cot_mid.at[g], own.at[1]),
-        pltpu.make_async_copy(right.at[pl.ds(g * share, share)], right_all.at[:, g], own.at[2]),
     ]
     for copy in local:
         copy.start()
-    mids, cots, rights = [], [], []
+    mids, cots = [], []
     for k in range(1, copies):
         q = lax.rem(g + k, copies)
         mids.append(remote(left.at[:, q], left_mid.at[g], mid_sems.at[0, k], mid_sems.at[1, k], (q, r)))
         cots.append(remote(cot.at[q], cot_mid.at[g], cot_sems.at[0, k], cot_sems.at[1, k], (q, r)))
-        rights.append(
-            remote(
-                right.at[pl.ds(q * share, share)], right_all.at[:, g],
-                right_sems.at[0, k], right_sems.at[1, k], (q, r),
-            )
-        )
-    for copy in mids + cots + rights:
+    for copy in mids + cots:
         copy.start()
     local[0].wait()
     for copy in mids:
@@ -93,27 +86,33 @@
             )
         )
         pairs[-1].start()
-    for copy in pairs + cot_rows + rights:
-        copy.wait_recv()
-    for copy in mids + cots + rights + along + pairs + cot_rows:
+    for copy in pairs + cot_rows:
+        copy.wait_recv()
+    for copy in mids + cots + along + pairs + cot_rows:
         copy.wait_send()
-    local[2].wait()
     keep.wait()
     keep_cot.wait()
 
 
 def collect(
     copies, rows, share,
-    back, matrix, right, right_out, left_out,
+    back, matrix, right, *refs,
+):
+    arrived, refs = refs[: copies - 1], refs[copies - 1 :]
+    (
+    right_out, left_out,
     factor, held_matrix, part, pair_in, chip_in, done,
     own, back_sems, pair_sems, row_sems, out_sems,
-):
+    ) = refs
     g, r, core, sibling = place(copies, rows)
     chips = rows // 2
     chip = r // 2
     loads = [
         pltpu.make_async_copy(matrix, held_matrix, own.at[0]),
-        pltpu.make_async_copy(right, factor, own.at[1]),
+        pltpu.make_async_copy(right.at[pl.ds(g * share, share)], factor.at[0], own.at[1]),
+    ] + [
+        pltpu.make_async_copy(arrived[k - 1], factor.at[k], own.at[3 + k])
+        for k in range(1, copies)
     ]
     for copy in loads:
         copy.start()
@@ -138,17 +137,19 @@
     for copy in loads:
         copy.wait()
     step = 16 if share % 16 == 0 else share
-    groups, tall = held_matrix.shape[1], held_matrix.shape[2]
+    groups, depth = held_matrix.shape[1], factor.shape[2]
     slab = part.shape[1:]
 
     def multiply(group, carry):
         for first in range(0, share, step):
-            product = lax.dot_general(
-                held_matrix[first : first + step, group],
-                factor[first : first + step],
-                (((2,), (1,)), ((0,), (0,))),
-                preferred_element_type=jnp.float32,
-            )
+            product = 0.0
+            for source in range(copies):
+                product = product + lax.dot_general(
+                    held_matrix[first : first + step, group, :, source * depth : (source + 1) * depth],
+                    factor[lax.rem(g + copies - source, copies), first : first + step],
+                    (((2,), (1,)), ((0,), (0,))),
+                    preferred_element_type=jnp.float32,
+                )
             turned = jnp.swapaxes(product.astype(part.dtype), 0, 1)
             part[pl.ds(group * (rows // groups), rows // groups), :, first : first + step, :] = (
                 turned.reshape(rows // groups, slab[0], step, slab[2])
@@ -214,6 +215,13 @@
     left_factor = (keep_both * opened * left_proj.astype(jnp.float32)).astype(bf16)
     left_in = left_factor.transpose(1, 0, 2).reshape(held, copies, share, length)
 
+    copy_here = lax.axis_index("copy")
+    arrived = []
+    for k in range(1, copies):
+        start = (copy_here + k) % copies * share
+        piece = lax.dynamic_slice_in_dim(right_factor, start, share)
+        arrived.append(lax.ppermute(piece, "copy", [(d, (d + k) % copies) for d in range(copies)]))
+
     size = held * share * block
     tall = -(-size // 2048) * 16
     cot = cotangent.reshape(copies, share, held, rows, block).transpose(0, 3, 2, 1, 4)
@@ -224,46 +232,42 @@
         return lambda *refs: body(copies, rows, share, *refs)
 
     chips = rows // 2
-    right, left, cot = pl.pallas_call(
+    left, cot = pl.pallas_call(
         kernel(spread),
         out_shape=(
-            jax.ShapeDtypeStruct((share, copies, block, length), bf16),
             jax.ShapeDtypeStruct((rows, copies, held, share, length), bf16),
             jax.ShapeDtypeStruct((rows, copies, tall, 128), bf16),
         ),
-        in_specs=[ANY] * 3,
-        out_specs=(ANY,) * 3,
+        in_specs=[ANY] * 2,
+        out_specs=(ANY,) * 2,
         scratch_shapes=[
             pltpu.VMEM((copies, held, share, length), bf16),
             pltpu.VMEM((copies, rows, tall, 128), bf16),
             sems(5),
             sems(2, copies),
             sems(2, copies),
-            sems(2, copies),
             sems(2, chips),
             sems(2, chips),
             sems(2, rows),
         ],
+        cost_estimate=pl.CostEstimate(flops=0, bytes_accessed=180_000_000, transcendentals=0),
         compiler_params=pltpu.CompilerParams(
             collective_id=0, has_side_effects=True, vmem_limit_bytes=8 << 20
         ),
-    )(right_factor, left_in, cot)
+    )(left_in, cot)
 
     cot = cot.reshape(rows, copies, tall * 128)[:, :, :size].reshape(rows, copies, held, share, block)
     cot = cot.transpose(3, 0, 1, 2, 4)
-    matrix = jnp.concatenate(
-        [
-            jnp.roll(cot, source, axis=2).reshape(share, rows * copies * held, block)
-            for source in range(copies)
-        ],
-        axis=2,
-    )
+    blocks = [
+        jnp.roll(cot, source, axis=2).reshape(share, rows * copies * held, block)
+        for source in range(copies)
+    ]
+    matrix = jnp.concatenate(blocks, axis=2)
     left = left.reshape(rows * copies * held, share, length).transpose(1, 0, 2)
     back = jnp.einsum("cij,cik->cjk", matrix, left, preferred_element_type=jnp.float32).astype(bf16)
     back = back.reshape(share, copies, block, length)
-    right = right.reshape(share, copies * block, length)
     groups = rows // 8 if rows % 8 == 0 else 1
-    grouped = matrix.reshape(share, groups, matrix.shape[1] // groups, copies * block)
+    grouped = matrix.reshape(share, groups, -1, copies * block)
 
     slab = (copies * held, share, length)
     slab_bytes = 2 * copies * held * share * length
@@ -273,16 +277,16 @@
             jax.ShapeDtypeStruct(right_factor.shape, bf16),
             jax.ShapeDtypeStruct((held, copies, share, length), bf16),
         ),
-        in_specs=[ANY] * 3,
+        in_specs=[ANY] * (copies + 2),
         out_specs=(ANY,) * 2,
         scratch_shapes=[
-            pltpu.VMEM(right.shape, bf16),
+            pltpu.VMEM((copies, share, block, length), bf16),
             pltpu.VMEM(grouped.shape, bf16),
             pltpu.VMEM((rows,) + slab, bf16),
             pltpu.VMEM((chips,) + slab, bf16),
             pltpu.VMEM((chips,) + slab, bf16),
             pltpu.VMEM((copies, held, share, length), bf16),
-            sems(4),
+            sems(3 + copies),
             sems(2, copies),
             sems(2, chips),
             sems(2, chips),
@@ -292,7 +296,7 @@
             collective_id=1, has_side_effects=True,
             vmem_limit_bytes=(24 << 20) + 2 * rows * slab_bytes,
         ),
-    )(back, grouped, right)
+    )(back, grouped, right_factor, *arrived)
 
     left_wide = left_sum.reshape(held, channels, length).transpose(1, 0, 2).astype(jnp.float32)
     grad_proj = (left_wide * keep_both * opened).astype(bf16)

time: 166 us -> 205 us (1.23)
  Pallas kernels: 130 us -> 167 us
  starting transfers between devices: 0 us -> 4.99 us
  other arithmetic: 7.76 us -> 5.39 us
    pallas_call x1, Pallas kernels: 70 us -> 105 us  [on_device(): pl.pallas_call(kernel(spread), out_shape=(jax.ShapeDtypeStruct((rows, cop...]
    ppermute x0 -> x3, starting transfers between devices: none -> 4.99 us  [on_device(): lax.ppermute(piece, 'copy', [(d, (d + k) % copies) for d in range(copies)])]
    unnamed x20 -> x26, local copies, waits for them, and re-layouts: 10.1 us -> 5.55 us
    dynamic_slice x0 -> x1, local copies, waits for them, and re-layouts: none -> 3.97 us  [on_device(): piece = lax.dynamic_slice_in_dim(right_factor, start, share)]
  transfers between devices with their start and end apart: 0 -> 3, of which waited for: 0 -> 0; matrix products, arithmetic and copies ran while one was open for 0% -> 10% of each run, Pallas kernels for 0% -> 51%
where the time goes in v3:
time: 205 us
  Pallas kernels  167 us (81%)
  local copies, waits for them, and re-layouts  19 us (9%)
  matrix products  7.42 us (4%)
  other arithmetic  5.39 us (3%)
  starting transfers between devices  4.99 us (2%)
    pallas_call x1, Pallas kernels, on_device(): pl.pallas_call(kernel(spread), out_shape=(jax.ShapeDtypeStruct((rows, cop...  105 us
    pallas_call x1, Pallas kernels, on_device(): pl.pallas_call(kernel(collect), out_shape=(jax.ShapeDtypeStruct(right_fac...  62 us
    dot_general x1, matrix products, on_device(): jnp.einsum('cij,cik->cjk', matrix, left, preferred_element_type=jnp.float32)  7.42 us
    unnamed x26, local copies, waits for them, and re-layouts  5.55 us
    ppermute x3, starting transfers between devices, on_device(): lax.ppermute(piece, 'copy', [(d, (d + k) % copies) for d in range(copies)])  4.99 us
  transfers between devices with their start and end apart: 3, of which 0 were waited for; matrix products, arithmetic and copies ran while one was open for 10% of the time, Pallas kernels for 51%

profile of v3, /device:TPU:0, one launch (start us, length us, event | category | flops | bytes accessed | tf_op | source)
XLA Modules:
  0.0 205.2 jit_solution(6560178556877210007)
XLA Ops:
  0.7 4.0 %constant_dynamic-slice_fusion = (bf16[32,48,384]{2,1,0:T(8,128)(2,1)}, bf16[32,48,384]{2,1,0:T(8,128)(2,1)}, bf16[32,48,384]{2,1,0:T(8,128)(2,1)}) fusion(bf16[128,48,384]{2,1,0:T(8,128)(2,1)} %refs_2_.1, s32[]{:T(128)S(6)} %select_n.33, s32[]{:T(128)S(6)} %select_n.31, s32[]{:T(128)S(6)} %select_n.29), kind=kLoop, calls=%fused_computation.22 | loop fusion | bytes 7077900 | tf_op jit(solution)/shard_map/dynamic_slice | solution.py:222
  4.7 3.9 %collective-permute-start.2 = (bf16[32,48,384]{2,1,0:T(8,128)(2,1)}, bf16[32,48,384]{2,1,0:T(8,128)(2,1)}, u32[]{:S(2)}, u32[]{:S(2)}) collective-permute-start(bf16[32,48,384]{2,1,0:T(8,128)(2,1)} %get-tuple-element.11), channel_id=1, source_target_pairs={{0,24},{8,0},{16,8},{24,16},{1,25},{9,1},{17,9},{25,17},{2,26},{10... | collective-permute-start | bytes 3538952 | tf_op jit(solution)/shard_map/ppermute | solution.py:223
  8.6 0.5 collective-permute-start.1
  9.1 0.6 collective-permute-start
  9.7 0.1 dynamic-slice_convert_fusion
  9.7 1.1 reshape.81
  10.9 0.3 copy.10
  11.1 2.6 %reshape.82 = bf16[4,8,7680]{2,1,0:T(8,128)(2,1)S(1)} reshape(bf16[4,8,5,32,48]{4,3,2,1,0:T(8,128)(2,1)S(1)} %copy.10) | data formatting | bytes 983040 | tf_op jit(solution)/shard_map/reshape | solution.py:228
  13.7 0.0 copy-start.4
  13.8 0.0 copy-start.5
  13.8 0.1 copy.30
  13.9 0.1 broadcast_multiply_fusion
  14.0 0.8 copy-done.4
  14.8 0.1 copy-done.5
  14.9 0.3 fusion.6
  15.2 105.4 %shard_map.76 = (bf16[8,4,5,32,384]{4,3,2,1,0:T(8,128)(2,1)S(1)}, bf16[8,4,64,128]{3,2,1,0:T(8,128)(2,1)S(1)}) custom-call(bf16[5,4,32,384]{3,2,1,0:T(8,128)(2,1)S(1)} %bitcast.48, bf16[4,8,64,128]{3,2,1,0:T(8,128)(2,1)S(1)} %copy.30), custom_call_target="tpu_custom_call" | custom-call | bytes 180000000 | tf_op jit(solution)/shard_map/pallas_call | solution.py:235
  120.6 0.0 copy-start
  120.6 1.9 copy-done
  122.6 0.1 reshape.84
  122.7 0.2 slice.34
  122.9 0.1 copy.21
  123.0 1.3 reshape.85
  124.3 0.3 copy.12
  124.7 0.3 fusion.16
  124.9 0.4 fusion.15
  125.3 0.5 copy.16
  125.8 0.3 pad_maximum_fusion.2
  126.1 0.3 copy.14
  126.4 0.5 copy.18
  126.9 0.5 pad_maximum_fusion.1
  127.5 0.3 copy.13
  127.7 0.5 copy.17
  128.3 0.3 copy.15
  128.5 0.5 copy.19
  129.1 0.2 copy-done.2
  129.3 2.7 %fusion.13.refs_1_ = bf16[32,1,160,192]{3,2,1,0:T(8,128)(2,1)S(1)} fusion(bf16[32,160,48]{2,1,0:T(8,128)(2,1)S(1)} %copy.19, bf16[32,160,48]{2,1,0:T(8,128)(2,1)S(1)} %copy.18, bf16[32,160,48]{2,1,0:T(8,128)(2,1)S(1)} %copy.17, bf16[32,160,48]{2,1,0:T(8,128)(2,1)S(1)} %copy.16), kind=kLoop, calls=%fused_computation.26 | loop fusion | flops 7864320 | bytes 3932160 | tf_op jit(solution)/shard_map/reshape | solution.py:270
  132.0 0.0 copy-done.3
  132.0 0.0 slice-start
  132.0 0.0 copy-done.1
  132.1 0.0 slice-start.1
  132.1 7.4 %fusion.3 = bf16[32,192,384]{2,1,0:T(8,128)(2,1)S(1)} fusion(bf16[160,32,384]{2,1,0:T(8,128)(2,1)S(1)} %bitcast.49, bf16[32,160,48]{2,1,0:T(8,128)(2,1)} %copy-done.3, bf16[32,160,48]{2,1,0:T(8,128)(2,1)S(1)} %copy.18, bf16[32,160,48]{2,1,0:T(8,128)(2,1)} %copy-done.2, bf16[32,160,48]{2,1,0:T(8,128)(2,1)S(1)} %copy.16), kind=kOutput, calls=%fused_computation.3 | convolution fusion | flops 765198336 | bytes 10616832 | tf_op jit(solution)/shard_map/cij,cik->cjk/dot_general | solution.py:267
  139.5 0.0 collective-permute-done.2.refs_5_
  139.5 0.0 collective-permute-done.1.refs_4_
  139.5 0.0 collective-permute-done.refs_3_
  139.5 0.0 copy-start.6
  139.6 62.0 %shard_map.77 = (bf16[128,48,384]{2,1,0:T(8,128)(2,1)S(1)}, bf16[5,4,32,384]{3,2,1,0:T(8,128)(2,1)S(1)}) custom-call(bf16[32,4,48,384]{3,2,1,0:T(8,128)(2,1)S(1)} %bitcast.47, bf16[32,1,160,192]{3,2,1,0:T(8,128)(2,1)S(1)} %fusion.13.refs_1_, bf16[128,48,384]{2,1,0:T(8,128)(2,1)S(1)} %bitcast.46, bf16[32,48,384]{2,1,0:T(8,128)(2,1)} %collective-permute-done.refs_3_, ...), custom_call_target="tpu_custom_call" | custom-call | tf_op jit(solution)/shard_map/pallas_call | solution.py:274
  201.5 1.5 fusion.9
  203.0 2.2 %copy.32 = bf16[128,48,384]{2,1,0:T(8,128)(2,1)} copy(bf16[128,48,384]{2,1,0:T(8,128)(2,1)S(1)} %get-tuple-element.29) | data formatting | bytes 9437184
  (14 shorter events, 0.1 us)
Async XLA Ops:
  0.7 9.0 %copy-start.8 = (s32[384]{0:T(512)S(1)}, s32[384]{0:T(512)}, u32[]{:S(2)}) copy-start(s32[384]{0:T(512)} %param.9) | copy-start | bytes 4612
  0.7 9.1 %copy-start.7 = (bf16[128,5,384]{2,0,1:T(8,128)(2,1)S(1)}, bf16[128,5,384]{2,0,1:T(8,128)(2,1)}, u32[]{:S(2)}) copy-start(bf16[128,5,384]{2,0,1:T(8,128)(2,1)} %param.8) | copy-start | bytes 1474564
  4.7 134.8 %collective-permute-start.2 = (bf16[32,48,384]{2,1,0:T(8,128)(2,1)}, bf16[32,48,384]{2,1,0:T(8,128)(2,1)}, u32[]{:S(2)}, u32[]{:S(2)}) collective-permute-start(bf16[32,48,384]{2,1,0:T(8,128)(2,1)} %get-tuple-element.11), channel_id=1, source_target_pairs={{0,24},{8,0},{16,8},{24,16},{1,25},{9,1},{17,9},{25,17},{2,26},{10... | collective-permute-start | bytes 3538952 | tf_op jit(solution)/shard_map/ppermute | solution.py:223
  8.6 130.9 %collective-permute-start.1 = (bf16[32,48,384]{2,1,0:T(8,128)(2,1)}, bf16[32,48,384]{2,1,0:T(8,128)(2,1)}, u32[]{:S(2)}, u32[]{:S(2)}) collective-permute-start(bf16[32,48,384]{2,1,0:T(8,128)(2,1)} %get-tuple-element.12), channel_id=1, source_target_pairs={{0,16},{8,24},{16,0},{24,8},{1,17},{9,25},{17,1},{25,9},{2,18},{10... | collective-permute-start | bytes 3538952 | tf_op jit(solution)/shard_map/ppermute | solution.py:223
  9.1 130.4 %collective-permute-start = (bf16[32,48,384]{2,1,0:T(8,128)(2,1)}, bf16[32,48,384]{2,1,0:T(8,128)(2,1)}, u32[]{:S(2)}, u32[]{:S(2)}) collective-permute-start(bf16[32,48,384]{2,1,0:T(8,128)(2,1)} %get-tuple-element.13), channel_id=1, source_target_pairs={{0,8},{8,16},{16,24},{24,0},{1,9},{9,17},{17,25},{25,1},{2,10},{10... | collective-permute-start | bytes 3538952 | tf_op jit(solution)/shard_map/ppermute | solution.py:223
  13.7 1.0 copy-start.4
  13.8 1.2 copy-start.5
  120.6 1.9 copy-start
  128.3 1.1 copy-start.2
  129.3 2.7 %copy-start.3 = (bf16[32,160,48]{2,1,0:T(8,128)(2,1)}, bf16[32,160,48]{2,1,0:T(8,128)(2,1)S(1)}, u32[]{:S(2)}) copy-start(bf16[32,160,48]{2,1,0:T(8,128)(2,1)S(1)} %copy.19) | copy-start | bytes 1474564
  129.3 2.7 %copy-start.1 = (bf16[8,4,5,32,384]{4,3,2,1,0:T(8,128)(2,1)S(1)}, bf16[8,4,5,32,384]{4,3,2,1,0:T(8,128)(2,1)}, u32[]{:S(2)}) copy-start(bf16[8,4,5,32,384]{4,3,2,1,0:T(8,128)(2,1)} %copy-done) | copy-start | bytes 11796484
  132.0 7.5 %slice-start = ((s8[4718592]{0:T(1024)(128)(4,1)}), s8[4194304]{0:T(1024)(128)(4,1)S(1)}, s32[]{:S(2)}) async-start(s8[4718592]{0:T(1024)(128)(4,1)} %bitcast.45), calls=%async_computation | async-start | bytes 8388608
  132.1 7.5 %slice-start.1 = ((s8[4718592]{0:T(1024)(128)(4,1)}), s8[524288]{0:T(1024)(128)(4,1)S(1)}, s32[]{:S(2)}) async-start(s8[4718592]{0:T(1024)(128)(4,1)} %bitcast.45), calls=%async_computation.1 | async-start | bytes 1048576
  139.5 62.0 %copy-start.6 = (bf16[128,5,384]{2,0,1:T(8,128)(2,1)S(1)}, bf16[128,5,384]{2,0,1:T(8,128)(2,1)}, u32[]{:S(2)}) copy-start(bf16[128,5,384]{2,0,1:T(8,128)(2,1)} %param.6) | copy-start | bytes 1474564
